TPU v7x, 256 devices: a whole 4x4x8 slice. The times are simulated.
256 devices in a mesh: leaf: 16 (over x, y), row: 16 (over z, core).
Axes of the slice: x: 4, y: 4, z: 8, core: 2. Of those that a mesh axis runs over, the one named last changes fastest.
Arguments:
- rhs: bfloat16 [6, 16, 512, 256], P(None, 'leaf', 'row'), may hold values from -6 to 6
- diag_inverse: bfloat16 [16, 6, 512, 512], P('leaf'), as said below
- factor: bfloat16 [16, 178, 512, 512], P('leaf', None, 'row'), as said below
- widths: int32 [6, 16], P(None, 'leaf'), may hold values from 64 to 512, as said below
- structure: int32 [16, 178], P('leaf'), may hold values from 0 to 1, as said below
Outputs:
- forward_solution: bfloat16 [6, 16, 512, 256], P(None, 'leaf', 'row')
- adjoint_solution: bfloat16 [6, 16, 512, 256], P(None, 'leaf', 'row')
Inputs may be any that keep to these rules, and one draw needn't show every extreme that they name: `widths`: every draw has a supernode of exactly 512 columns and one of exactly one eighth of 512 columns. `structure`: 1 where the block is present. Each diag_inverse[j, l] is lower triangular with diagonal entries from 0.5 to 1. `factor`: dense blocks of independent entries.
All inputs are finite; a program needn't handle non-finite values.
Results may differ from a plain program's by a relative error of at most 0.017.
Values may be sent and summed in bfloat16 or wider, within the bound.
A program may use at most 64 MiB of HBM per device.

v0:
```python
import jax
import jax.numpy as jnp
from jax import lax
from jax.sharding import PartitionSpec as P


def group_size(level_now, leaf_count):
    return min(2**level_now, leaf_count)


def block_offsets(levels, leaf_count):
    offset_table = {}
    cursor = 0
    for source_level in range(levels):
        for target_level in range(source_level + 1, levels):
            offset_table[source_level, target_level] = cursor
            cursor += group_size(target_level, leaf_count)
    return offset_table


def blocks_after(level_now, levels, leaf_count):
    return sum(
        (group_size(target_level, leaf_count) for target_level in range(level_now + 1, levels))
    )


def contract_rows(left_side, right_side):
    return lax.dot_general(
        left_side, right_side, (((0,), (0,)), ((), ())), preferred_element_type=jnp.float32
    )


def apply_columns(matrix, shard_piece):
    return jnp.dot(matrix, shard_piece, preferred_element_type=jnp.float32)


def group_reduce(partials, group_span, leaf_count, leaf_index):
    group_base = leaf_index // group_span * group_span
    spread = jnp.zeros((leaf_count,) + partials.shape[1:], jnp.float32)
    spread = lax.dynamic_update_slice_in_dim(spread, partials, group_base, 0)
    return lax.psum_scatter(
        spread.astype(jnp.bfloat16), "leaf", scatter_dimension=0, tiled=True
    ).astype(jnp.float32)[0]


def group_collect(own_block, group_span, leaf_index):
    everyone = lax.all_gather(own_block[None], "leaf", axis=0, tiled=True)
    group_base = leaf_index // group_span * group_span
    return lax.dynamic_slice_in_dim(everyone, group_base, group_span, 0)


def adjoint_level(flat_blocks, flat_values, own_full, full_mask, block_mask, inverse_cols):
    pulled = lax.psum(contract_rows(flat_blocks, flat_values).astype(jnp.bfloat16), "row").astype(
        jnp.float32
    )
    reduced_full = (full_mask[:, None] * (own_full.astype(jnp.float32) - pulled)).astype(
        jnp.bfloat16
    )
    solved = contract_rows(inverse_cols, reduced_full)
    return (block_mask[:, None] * solved).astype(jnp.bfloat16)


def shards(rhs, diag_inverse, factor, widths, structure):
    leaf_count = lax.axis_size("leaf")
    leaf_index = lax.axis_index("leaf")
    row_index = lax.axis_index("row")
    levels = rhs.shape[0]
    block_rows = rhs.shape[2]
    columns = rhs.shape[3]
    full_width = factor.shape[3]
    inverse = diag_inverse[0]
    blocks = factor[0]
    weights = structure[0].astype(jnp.float32)
    own_rows = row_index * block_rows
    positions = jnp.arange(full_width, dtype=jnp.int32)
    full_masks = (positions[None, :] < widths).astype(jnp.float32)
    block_masks = lax.dynamic_slice_in_dim(full_masks, own_rows, block_rows, 1)
    offset_table = block_offsets(levels, leaf_count)
    pending = {}
    for target_level in range(1, levels):
        pending[target_level] = jnp.zeros(
            (group_size(target_level, leaf_count), block_rows, columns), jnp.float32
        )
    forward_blocks = []
    forward_full = []
    for level_now in range(levels):
        if level_now > 0:
            incoming = group_reduce(
                pending[level_now], group_size(level_now, leaf_count), leaf_count, leaf_index
            )
        else:
            incoming = jnp.zeros((block_rows, columns), jnp.float32)
        residual = (
            block_masks[level_now][:, None] * (rhs[level_now, 0].astype(jnp.float32) - incoming)
        ).astype(jnp.bfloat16)
        solve_rows = inverse[level_now]
        folded = apply_columns(solve_rows, lax.all_gather(residual, "row", axis=0, tiled=True))
        solved_full = (full_masks[level_now][:, None] * folded).astype(jnp.bfloat16)
        solved_block = lax.dynamic_slice_in_dim(solved_full, own_rows, block_rows, 0)
        forward_blocks.append(solved_block)
        forward_full.append(solved_full)
        if level_now + 1 < levels:
            first_block = offset_table[level_now, level_now + 1]
            block_count = blocks_after(level_now, levels, leaf_count)
            chosen = blocks[first_block : first_block + block_count].reshape(
                block_count * block_rows, full_width
            )
            products = jnp.dot(chosen, solved_full, preferred_element_type=jnp.float32).reshape(
                block_count, block_rows, columns
            )
            products = products * weights[first_block : first_block + block_count][:, None, None]
            cursor = 0
            for target_level in range(level_now + 1, levels):
                group_span = group_size(target_level, leaf_count)
                pending[target_level] = (
                    pending[target_level] + products[cursor : cursor + group_span]
                )
                cursor += group_span
    gathered = {}
    adjoint_blocks = [None] * levels
    for level_now in reversed(range(levels)):
        inverse_cols = lax.dynamic_slice_in_dim(inverse[level_now], own_rows, block_rows, 1)
        if level_now + 1 == levels:
            solved = contract_rows(inverse_cols, forward_full[level_now])
            own_adjoint = (block_masks[level_now][:, None] * solved).astype(jnp.bfloat16)
        else:
            first_block = offset_table[level_now, level_now + 1]
            block_count = blocks_after(level_now, levels, leaf_count)
            stacked = jnp.concatenate(
                [gathered[upper_level] for upper_level in range(level_now + 1, levels)], 0
            )
            stacked = stacked * structure[0, first_block : first_block + block_count][
                :, None, None
            ].astype(jnp.bfloat16)
            flat_blocks = blocks[first_block : first_block + block_count].reshape(
                block_count * block_rows, full_width
            )
            flat_values = stacked.reshape(block_count * block_rows, columns)
            own_adjoint = adjoint_level(
                flat_blocks,
                flat_values,
                forward_full[level_now],
                full_masks[level_now],
                block_masks[level_now],
                inverse_cols,
            )
        adjoint_blocks[level_now] = own_adjoint
        if level_now > 0:
            gathered[level_now] = group_collect(
                own_adjoint, group_size(level_now, leaf_count), leaf_index
            )
    return (jnp.stack(forward_blocks)[:, None], jnp.stack(adjoint_blocks)[:, None])


def solution(mesh):
    placed = (
        P(None, "leaf", "row", None),
        P("leaf", None, None, None),
        P("leaf", None, "row", None),
        P(None, "leaf"),
        P("leaf", None),
    )
    return jax.shard_map(
        shards,
        mesh=mesh,
        in_specs=placed,
        out_specs=(P(None, "leaf", "row", None), P(None, "leaf", "row", None)),
        check_vma=False,
    )
```

profile of v0, /device:TPU:1, one launch (start us, length us, event | category | flops | bytes accessed | tf_op | source)
XLA Modules:
  0.0 1223.9 jit_solution(11152830773635222627)
XLA Ops:
  8.9 22.0 %all_gather.33 = bf16[512,256]{1,0:T(8,128)(2,1)S(1)} all-gather(bf16[32,256]{1,0:T(8,128)(2,1)S(1)} %fusion.72), channel_id=1, replica_groups=mesh['leaf'=16,'row'=16] {'row'}, dimensions={0}, use_global_device_ids=true | all-gather | bytes 278528 | tf_op jit(solution)/shard_map/all_gather | solution.py:97
  38.4 71.6 %reduce-scatter.16.cloned.1.call-done = bf16[1,32,256]{2,1,0:T(8,128)(2,1)} async-done(((bf16[16,32,256]{2,1,0:T(8,128)(2,1)}), bf16[1,32,256]{2,1,0:T(8,128)(2,1)}) %reduce-scatter.16.cloned.1.call-update) | async-done | bytes 16400
  110.8 20.2 %all_gather.34 = bf16[512,256]{1,0:T(8,128)(2,1)S(1)} all-gather(bf16[32,256]{1,0:T(8,128)(2,1)S(1)} %fusion.71), channel_id=1, replica_groups=mesh['leaf'=16,'row'=16] {'row'}, dimensions={0}, use_global_device_ids=true | all-gather | bytes 278528 | tf_op jit(solution)/shard_map/all_gather | solution.py:97
  134.8 2.9 copy.19
  144.7 69.2 %reduce-scatter.18.cloned.1.call-done = bf16[1,32,256]{2,1,0:T(8,128)(2,1)} async-done(((bf16[16,32,256]{2,1,0:T(8,128)(2,1)}), bf16[1,32,256]{2,1,0:T(8,128)(2,1)}) %reduce-scatter.18.cloned.1.call-update) | async-done | bytes 16400
  214.8 20.3 %all_gather.35 = bf16[512,256]{1,0:T(8,128)(2,1)S(1)} all-gather(bf16[32,256]{1,0:T(8,128)(2,1)S(1)} %fusion.69), channel_id=1, replica_groups=mesh['leaf'=16,'row'=16] {'row'}, dimensions={0}, use_global_device_ids=true | all-gather | bytes 278528 | tf_op jit(solution)/shard_map/all_gather | solution.py:97
  238.8 2.8 copy.20
  248.5 69.3 %reduce-scatter.20.cloned.1.call-done = bf16[1,32,256]{2,1,0:T(8,128)(2,1)} async-done(((bf16[16,32,256]{2,1,0:T(8,128)(2,1)}), bf16[1,32,256]{2,1,0:T(8,128)(2,1)}) %reduce-scatter.20.cloned.1.call-update) | async-done | bytes 16400
  318.6 20.2 %all_gather.36 = bf16[512,256]{1,0:T(8,128)(2,1)S(1)} all-gather(bf16[32,256]{1,0:T(8,128)(2,1)S(1)} %fusion.67), channel_id=1, replica_groups=mesh['leaf'=16,'row'=16] {'row'}, dimensions={0}, use_global_device_ids=true | all-gather | bytes 278528 | tf_op jit(solution)/shard_map/all_gather | solution.py:97
  352.1 69.4 %reduce-scatter.22.cloned.1.call-done = bf16[1,32,256]{2,1,0:T(8,128)(2,1)} async-done(((bf16[16,32,256]{2,1,0:T(8,128)(2,1)}), bf16[1,32,256]{2,1,0:T(8,128)(2,1)}) %reduce-scatter.22.cloned.1.call-update) | async-done | bytes 16400
  422.3 20.3 %all_gather.37 = bf16[512,256]{1,0:T(8,128)(2,1)S(1)} all-gather(bf16[32,256]{1,0:T(8,128)(2,1)S(1)} %fusion.65), channel_id=1, replica_groups=mesh['leaf'=16,'row'=16] {'row'}, dimensions={0}, use_global_device_ids=true | all-gather | bytes 278528 | tf_op jit(solution)/shard_map/all_gather | solution.py:97
  451.1 3.5 fusion.86
  454.7 67.7 %reduce-scatter.24.cloned.1.call-done = bf16[1,32,256]{2,1,0:T(8,128)(2,1)} async-done(((bf16[16,32,256]{2,1,0:T(8,128)(2,1)}), bf16[1,32,256]{2,1,0:T(8,128)(2,1)}) %reduce-scatter.24.cloned.1.call-update) | async-done | bytes 16400
  523.2 20.2 %all_gather.38 = bf16[512,256]{1,0:T(8,128)(2,1)S(1)} all-gather(bf16[32,256]{1,0:T(8,128)(2,1)S(1)} %fusion.63), channel_id=1, replica_groups=mesh['leaf'=16,'row'=16] {'row'}, dimensions={0}, use_global_device_ids=true | all-gather | bytes 278528 | tf_op jit(solution)/shard_map/all_gather | solution.py:97
  546.1 18.0 %all-gather = bf16[512,256]{1,0:T(8,128)(2,1)S(1)} all-gather(bf16[32,256]{1,0:T(8,128)(2,1)S(1)} %fusion.11), channel_id=2, replica_groups=mesh['leaf'=16,'row'=16] {'leaf'}, dimensions={0}, use_global_device_ids=true | all-gather | bytes 278528 | tf_op jit(solution)/shard_map/all_gather | solution.py:47
  569.0 105.7 %all-reduce.11.cloned.1.call-done = bf16[512,256]{0,1:T(8,128)(2,1)} async-done(((bf16[512,256]{0,1:T(8,128)(2,1)}), bf16[512,256]{0,1:T(8,128)(2,1)}) %all-reduce.11.cloned.1.call-update) | async-done | bytes 262160 | tf_op jit(solution)/shard_map/psum | solution.py:53
  676.1 18.5 %all-gather.1 = bf16[512,256]{1,0:T(8,128)(2,1)S(1)} all-gather(bf16[32,256]{1,0:T(8,128)(2,1)S(1)} %fusion.12), channel_id=3, replica_groups=mesh['leaf'=16,'row'=16] {'leaf'}, dimensions={0}, use_global_device_ids=true | all-gather | bytes 278528 | tf_op jit(solution)/shard_map/all_gather | solution.py:47
  699.9 109.0 %all-reduce.13.cloned.1.call-done = bf16[512,256]{0,1:T(8,128)(2,1)} async-done(((bf16[512,256]{0,1:T(8,128)(2,1)}), bf16[512,256]{0,1:T(8,128)(2,1)}) %all-reduce.13.cloned.1.call-update) | async-done | bytes 262160 | tf_op jit(solution)/shard_map/psum | solution.py:53
  810.4 18.5 %all-gather.2 = bf16[512,256]{1,0:T(8,128)(2,1)S(1)} all-gather(bf16[32,256]{1,0:T(8,128)(2,1)S(1)} %fusion.13), channel_id=4, replica_groups=mesh['leaf'=16,'row'=16] {'leaf'}, dimensions={0}, use_global_device_ids=true | all-gather | bytes 278528 | tf_op jit(solution)/shard_map/all_gather | solution.py:47
  837.5 107.2 %all-reduce.15.cloned.1.call-done = bf16[512,256]{0,1:T(8,128)(2,1)} async-done(((bf16[512,256]{0,1:T(8,128)(2,1)}), bf16[512,256]{0,1:T(8,128)(2,1)}) %all-reduce.15.cloned.1.call-update) | async-done | bytes 262160 | tf_op jit(solution)/shard_map/psum | solution.py:53
  946.1 18.7 %all-gather.3 = bf16[512,256]{1,0:T(8,128)(2,1)S(1)} all-gather(bf16[32,256]{1,0:T(8,128)(2,1)S(1)} %fusion.14), channel_id=5, replica_groups=mesh['leaf'=16,'row'=16] {'leaf'}, dimensions={0}, use_global_device_ids=true | all-gather | bytes 278528 | tf_op jit(solution)/shard_map/all_gather | solution.py:47
  969.6 110.7 %all-reduce.17.cloned.1.call-done = bf16[512,256]{0,1:T(8,128)(2,1)} async-done(((bf16[512,256]{0,1:T(8,128)(2,1)}), bf16[512,256]{0,1:T(8,128)(2,1)}) %all-reduce.17.cloned.1.call-update) | async-done | bytes 262160 | tf_op jit(solution)/shard_map/psum | solution.py:53
  1081.7 18.5 %all-gather.4 = bf16[512,256]{1,0:T(8,128)(2,1)S(1)} all-gather(bf16[32,256]{1,0:T(8,128)(2,1)S(1)} %fusion.15), channel_id=6, replica_groups=mesh['leaf'=16,'row'=16] {'leaf'}, dimensions={0}, use_global_device_ids=true | all-gather | bytes 278528 | tf_op jit(solution)/shard_map/all_gather | solution.py:47
  1103.9 111.1 %all-reduce.19.cloned.1.call-done = bf16[512,256]{0,1:T(8,128)(2,1)} async-done(((bf16[512,256]{0,1:T(8,128)(2,1)}), bf16[512,256]{0,1:T(8,128)(2,1)}) %all-reduce.19.cloned.1.call-update) | async-done | bytes 262160 | tf_op jit(solution)/shard_map/psum | solution.py:53
  (210 shorter events, 93.4 us)
Async XLA Ops:
  7.2 102.8 %reduce-scatter.16.cloned.1.call-start = ((), (), s32[]{:S(2)}) async-start(), calls=%async_computation.10 | async-start | bytes 278528
  8.0 123.0 %copy-start.33 = (f32[1,512]{1,0:T(1,128)}, f32[1,512]{1,0:T(1,128)S(1)}, u32[]{:S(2)}) copy-start(f32[1,512]{1,0:T(1,128)S(1)} %get-tuple-element.18) | copy-start | bytes 6148
  8.0 227.1 %copy-start.35 = (f32[1,512]{1,0:T(1,128)}, f32[1,512]{1,0:T(1,128)S(1)}, u32[]{:S(2)}) copy-start(f32[1,512]{1,0:T(1,128)S(1)} %get-tuple-element.17) | copy-start | bytes 6148
  8.0 330.9 %copy-start.36 = (f32[1,512]{1,0:T(1,128)}, f32[1,512]{1,0:T(1,128)S(1)}, u32[]{:S(2)}) copy-start(f32[1,512]{1,0:T(1,128)S(1)} %get-tuple-element.16) | copy-start | bytes 6148
  8.0 434.6 %copy-start.37 = (f32[1,512]{1,0:T(1,128)}, f32[1,512]{1,0:T(1,128)S(1)}, u32[]{:S(2)}) copy-start(f32[1,512]{1,0:T(1,128)S(1)} %get-tuple-element.15) | copy-start | bytes 6148
  8.1 205.8 %copy-start.42 = (f32[32]{0:T(128)}, f32[32]{0:T(128)S(1)}, u32[]{:S(2)}) copy-start(f32[32]{0:T(128)S(1)} %get-tuple-element.23) | copy-start | bytes 388
  8.1 309.6 %copy-start.43 = (f32[32]{0:T(128)}, f32[32]{0:T(128)S(1)}, u32[]{:S(2)}) copy-start(f32[32]{0:T(128)S(1)} %get-tuple-element.22) | copy-start | bytes 388
  8.1 413.4 %copy-start.44 = (f32[32]{0:T(128)}, f32[32]{0:T(128)S(1)}, u32[]{:S(2)}) copy-start(f32[32]{0:T(128)S(1)} %get-tuple-element.21) | copy-start | bytes 388
  36.7 177.2 %reduce-scatter.18.cloned.1.call-start = ((), (), s32[]{:S(2)}) async-start(), calls=%async_computation.11 | async-start | bytes 278528
  142.0 175.7 %reduce-scatter.20.cloned.1.call-start = ((), (), s32[]{:S(2)}) async-start(), calls=%async_computation.12 | async-start | bytes 278528
  245.9 175.6 %reduce-scatter.22.cloned.1.call-start = ((), (), s32[]{:S(2)}) async-start(), calls=%async_computation.13 | async-start | bytes 278528
  349.7 172.6 %reduce-scatter.24.cloned.1.call-start = ((), (), s32[]{:S(2)}) async-start(), calls=%async_computation.14 | async-start | bytes 278528
  450.5 224.2 %all-reduce.11.cloned.1.call-start = ((), (), s32[]{:S(2)}) async-start(), calls=%async_computation.5 | async-start | bytes 524288 | tf_op jit(solution)/shard_map/psum | solution.py:53
  544.8 129.9 %copy-start.14 = (bf16[256,512]{1,0:T(8,128)(2,1)S(1)}, bf16[256,512]{1,0:T(8,128)(2,1)}, u32[]{:S(2)}) copy-start(bf16[256,512]{1,0:T(8,128)(2,1)} %copy-done.13) | copy-start | bytes 786436
  565.2 243.7 %all-reduce.13.cloned.1.call-start = ((), (), s32[]{:S(2)}) async-start(), calls=%async_computation.6 | async-start | bytes 524288 | tf_op jit(solution)/shard_map/psum | solution.py:53
  696.5 248.2 %all-reduce.15.cloned.1.call-start = ((), (), s32[]{:S(2)}) async-start(), calls=%async_computation.7 | async-start | bytes 524288 | tf_op jit(solution)/shard_map/psum | solution.py:53
  832.3 248.0 %all-reduce.17.cloned.1.call-start = ((), (), s32[]{:S(2)}) async-start(), calls=%async_computation.8 | async-start | bytes 524288 | tf_op jit(solution)/shard_map/psum | solution.py:53
  967.8 133.2 %copy-start.19 = (bf16[512,256]{1,0:T(8,128)(2,1)S(1)}, bf16[512,256]{1,0:T(8,128)(2,1)}, u32[]{:S(2)}) copy-start(bf16[512,256]{1,0:T(8,128)(2,1)} %copy-done.18) | copy-start | bytes 786436
  967.9 133.2 %copy-start.47 = (bf16[46]{0:T(256)(128)(2,1)S(1)}, bf16[46]{0:T(256)(128)(2,1)}, u32[]{:S(2)}) copy-start(bf16[46]{0:T(256)(128)(2,1)} %slice_bitcast_fusion) | copy-start | bytes 280
  967.9 247.1 %all-reduce.19.cloned.1.call-start = ((), (), s32[]{:S(2)}) async-start(), calls=%async_computation.9 | async-start | bytes 524288 | tf_op jit(solution)/shard_map/psum | solution.py:53
  1101.2 113.8 %copy-start.11 = (bf16[256,512]{1,0:T(8,128)(2,1)S(1)}, bf16[256,512]{1,0:T(8,128)(2,1)}, u32[]{:S(2)}) copy-start(bf16[256,512]{1,0:T(8,128)(2,1)} %copy-done.10) | copy-start | bytes 786436
  1101.2 113.8 %copy-start.32 = (f32[1,512]{1,0:T(1,128)S(1)}, f32[1,512]{1,0:T(1,128)}, u32[]{:S(2)}) copy-start(f32[1,512]{1,0:T(1,128)} %copy-done.31) | copy-start | bytes 6148
  1101.3 115.1 %copy-start.28 = (bf16[32,256]{1,0:T(8,128)(2,1)S(1)}, bf16[32,256]{1,0:T(8,128)(2,1)}, u32[]{:S(2)}) copy-start(bf16[32,256]{1,0:T(8,128)(2,1)} %copy-done.27) | copy-start | bytes 49156
  1101.3 115.1 %copy-start.26 = (bf16[32,256]{1,0:T(8,128)(2,1)S(1)}, bf16[32,256]{1,0:T(8,128)(2,1)}, u32[]{:S(2)}) copy-start(bf16[32,256]{1,0:T(8,128)(2,1)} %copy-done.25) | copy-start | bytes 49156
  (34 other events, 843.0 us)
Sparse Core Ops, SparseCore 0:
  36.8 73.0 reduce-scatter.15
  142.2 71.6 reduce-scatter.17
  246.1 71.6 reduce-scatter.19
  349.8 71.6 reduce-scatter.21
  450.6 71.6 reduce-scatter.23
  565.4 109.3 all-reduce.10
  696.6 112.2 all-reduce.12
  832.4 112.2 all-reduce.14
  968.0 112.2 all-reduce.16
  1102.7 112.2 all-reduce.18
where the time goes:
time: 1230 us; the launch traced here: 1220 us
  waiting for transfers between devices  891 us (72%)
  blocking collectives  215 us (17%)
  local copies, waits for them, and re-layouts  53.4 us (4%)
  matrix products  29 us (2%)
  other arithmetic  19.6 us (2%)
  between operations  15 us (1%)
    psum x5, waiting for transfers between devices, adjoint_level(): lax.psum(contract_rows(flat_blocks, flat_values).astype(jnp.bfloat16), 'r...  544 us
    unnamed x15, waiting for transfers between devices  347 us
    all_gather x6, blocking collectives, shards(): lax.all_gather(residual, 'row', axis=0, tiled=True)  123 us
    all_gather x5, blocking collectives, group_collect(): everyone = lax.all_gather(own_block[None], 'leaf', axis=0, tiled=True)  92.2 us
  transfers between devices with their start and end apart: 10, of which 10 were waited for; matrix products, arithmetic and copies ran while one was open for 2% of the time, Pallas kernels for 0%

commit v1 on v0

--- a/solution.py
+++ b/solution.py
@@ -2,6 +2,11 @@
 import jax.numpy as jnp
 from jax import lax
 from jax.sharding import PartitionSpec as P
+
+
+def summed_here(x, axis):
+    pieces = lax.all_gather(x, axis)
+    return jnp.sum(pieces, axis=0)
 
 
 def group_size(level_now, leaf_count):
@@ -50,9 +55,9 @@
 
 
 def adjoint_level(flat_blocks, flat_values, own_full, full_mask, block_mask, inverse_cols):
-    pulled = lax.psum(contract_rows(flat_blocks, flat_values).astype(jnp.bfloat16), "row").astype(
-        jnp.float32
-    )
+    pulled = summed_here(
+        contract_rows(flat_blocks, flat_values).astype(jnp.bfloat16), "row"
+    ).astype(jnp.float32)
     reduced_full = (full_mask[:, None] * (own_full.astype(jnp.float32) - pulled)).astype(
         jnp.bfloat16
     )

time: 1230 us -> 923 us (0.75)
  waiting for transfers between devices: 891 us -> 565 us
    psum x5 -> x0, waiting for transfers between devices: 544 us -> none  [adjoint_level(): lax.psum(contract_rows(flat_blocks, flat_values).astype(jnp.bfloat16), 'r...]
    all_gather x0 -> x5, waiting for transfers between devices: none -> 216 us  [summed_here(): pieces = lax.all_gather(x, axis)]
    unnamed x109 -> x104, local copies, waits for them, and re-layouts: 18.2 us -> 33.2 us
    reduce_sum x0 -> x5, other arithmetic: none -> 12.7 us  [summed_here(): return jnp.sum(pieces, axis=0)]
where the time goes in v1:
time: 923 us; the launch traced here: 915 us
  waiting for transfers between devices  565 us (61%)
  blocking collectives  216 us (23%)
  local copies, waits for them, and re-layouts  59.9 us (6%)
  other arithmetic  30.2 us (3%)
  matrix products  27.2 us (3%)
  between operations  15.3 us (2%)
    unnamed x15, waiting for transfers between devices  349 us
    all_gather x5, waiting for transfers between devices, summed_here(): pieces = lax.all_gather(x, axis)  216 us
    all_gather x6, blocking collectives, shards(): lax.all_gather(residual, 'row', axis=0, tiled=True)  123 us
    all_gather x5, blocking collectives, group_collect(): everyone = lax.all_gather(own_block[None], 'leaf', axis=0, tiled=True)  92.4 us
    unnamed x104, local copies, waits for them, and re-layouts  33.2 us
  transfers between devices with their start and end apart: 10, of which 10 were waited for; matrix products, arithmetic and copies ran while one was open for 2% of the time, Pallas kernels for 0%

profile of v1, /device:TPU:1, one launch (start us, length us, event | category | flops | bytes accessed | tf_op | source)
XLA Modules:
  0.0 914.6 jit_solution(9649019794852929918)
XLA Ops:
  8.9 22.0 %all_gather.63 = bf16[512,256]{1,0:T(8,128)(2,1)S(1)} all-gather(bf16[32,256]{1,0:T(8,128)(2,1)S(1)} %fusion.72), channel_id=1, replica_groups=mesh['leaf'=16,'row'=16] {'row'}, dimensions={0}, use_global_device_ids=true | all-gather | bytes 278528 | tf_op jit(solution)/shard_map/all_gather | solution.py:102
  38.3 71.6 %reduce-scatter.16.cloned.1.call-done = bf16[1,32,256]{2,1,0:T(8,128)(2,1)} async-done(((bf16[16,32,256]{2,1,0:T(8,128)(2,1)}), bf16[1,32,256]{2,1,0:T(8,128)(2,1)}) %reduce-scatter.16.cloned.1.call-update) | async-done | bytes 16400
  110.7 20.2 %all_gather.64 = bf16[512,256]{1,0:T(8,128)(2,1)S(1)} all-gather(bf16[32,256]{1,0:T(8,128)(2,1)S(1)} %fusion.71), channel_id=1, replica_groups=mesh['leaf'=16,'row'=16] {'row'}, dimensions={0}, use_global_device_ids=true | all-gather | bytes 278528 | tf_op jit(solution)/shard_map/all_gather | solution.py:102
  144.6 69.2 %reduce-scatter.18.cloned.1.call-done = bf16[1,32,256]{2,1,0:T(8,128)(2,1)} async-done(((bf16[16,32,256]{2,1,0:T(8,128)(2,1)}), bf16[1,32,256]{2,1,0:T(8,128)(2,1)}) %reduce-scatter.18.cloned.1.call-update) | async-done | bytes 16400
  214.7 20.2 %all_gather.65 = bf16[512,256]{1,0:T(8,128)(2,1)S(1)} all-gather(bf16[32,256]{1,0:T(8,128)(2,1)S(1)} %fusion.69), channel_id=1, replica_groups=mesh['leaf'=16,'row'=16] {'row'}, dimensions={0}, use_global_device_ids=true | all-gather | bytes 278528 | tf_op jit(solution)/shard_map/all_gather | solution.py:102
  248.5 69.4 %reduce-scatter.20.cloned.1.call-done = bf16[1,32,256]{2,1,0:T(8,128)(2,1)} async-done(((bf16[16,32,256]{2,1,0:T(8,128)(2,1)}), bf16[1,32,256]{2,1,0:T(8,128)(2,1)}) %reduce-scatter.20.cloned.1.call-update) | async-done | bytes 16400
  318.7 20.2 %all_gather.66 = bf16[512,256]{1,0:T(8,128)(2,1)S(1)} all-gather(bf16[32,256]{1,0:T(8,128)(2,1)S(1)} %fusion.67), channel_id=1, replica_groups=mesh['leaf'=16,'row'=16] {'row'}, dimensions={0}, use_global_device_ids=true | all-gather | bytes 278528 | tf_op jit(solution)/shard_map/all_gather | solution.py:102
  350.9 70.6 %reduce-scatter.22.cloned.1.call-done = bf16[1,32,256]{2,1,0:T(8,128)(2,1)} async-done(((bf16[16,32,256]{2,1,0:T(8,128)(2,1)}), bf16[1,32,256]{2,1,0:T(8,128)(2,1)}) %reduce-scatter.22.cloned.1.call-update) | async-done | bytes 16400
  422.4 20.3 %all_gather.67 = bf16[512,256]{1,0:T(8,128)(2,1)S(1)} all-gather(bf16[32,256]{1,0:T(8,128)(2,1)S(1)} %fusion.65), channel_id=1, replica_groups=mesh['leaf'=16,'row'=16] {'row'}, dimensions={0}, use_global_device_ids=true | all-gather | bytes 278528 | tf_op jit(solution)/shard_map/all_gather | solution.py:102
  454.0 68.3 %reduce-scatter.24.cloned.1.call-done = bf16[1,32,256]{2,1,0:T(8,128)(2,1)} async-done(((bf16[16,32,256]{2,1,0:T(8,128)(2,1)}), bf16[1,32,256]{2,1,0:T(8,128)(2,1)}) %reduce-scatter.24.cloned.1.call-update) | async-done | bytes 16400
  523.2 20.2 %all_gather.68 = bf16[512,256]{1,0:T(8,128)(2,1)S(1)} all-gather(bf16[32,256]{1,0:T(8,128)(2,1)S(1)} %fusion.63), channel_id=1, replica_groups=mesh['leaf'=16,'row'=16] {'row'}, dimensions={0}, use_global_device_ids=true | all-gather | bytes 278528 | tf_op jit(solution)/shard_map/all_gather | solution.py:102
  545.1 18.0 %all-gather = bf16[512,256]{1,0:T(8,128)(2,1)S(1)} all-gather(bf16[32,256]{1,0:T(8,128)(2,1)S(1)} %fusion.11), channel_id=2, replica_groups=mesh['leaf'=16,'row'=16] {'leaf'}, dimensions={0}, use_global_device_ids=true | all-gather | bytes 278528 | tf_op jit(solution)/shard_map/all_gather | solution.py:52
  564.8 42.9 %all-gather.16.cloned.1.call-done = bf16[8192,256]{0,1:T(8,128)(2,1)} async-done(((bf16[512,256]{0,1:T(8,128)(2,1)}), bf16[8192,256]{0,1:T(8,128)(2,1)}) %all-gather.16.cloned.1.call-update) | async-done | bytes 4194320 | tf_op jit(solution)/shard_map/all_gather | solution.py:8
  607.7 4.0 copy.31
  615.6 18.6 %all-gather.2 = bf16[512,256]{1,0:T(8,128)(2,1)S(1)} all-gather(bf16[32,256]{1,0:T(8,128)(2,1)S(1)} %fusion.12), channel_id=4, replica_groups=mesh['leaf'=16,'row'=16] {'leaf'}, dimensions={0}, use_global_device_ids=true | all-gather | bytes 278528 | tf_op jit(solution)/shard_map/all_gather | solution.py:52
  635.6 44.1 %all-gather.18.cloned.1.call-done = bf16[8192,256]{0,1:T(8,128)(2,1)} async-done(((bf16[512,256]{0,1:T(8,128)(2,1)}), bf16[8192,256]{0,1:T(8,128)(2,1)}) %all-gather.18.cloned.1.call-update) | async-done | bytes 4194320 | tf_op jit(solution)/shard_map/all_gather | solution.py:8
  679.7 4.0 copy.32
  687.6 18.6 %all-gather.4 = bf16[512,256]{1,0:T(8,128)(2,1)S(1)} all-gather(bf16[32,256]{1,0:T(8,128)(2,1)S(1)} %fusion.13), channel_id=6, replica_groups=mesh['leaf'=16,'row'=16] {'leaf'}, dimensions={0}, use_global_device_ids=true | all-gather | bytes 278528 | tf_op jit(solution)/shard_map/all_gather | solution.py:52
  709.8 43.4 %all-gather.20.cloned.1.call-done = bf16[8192,256]{0,1:T(8,128)(2,1)} async-done(((bf16[512,256]{0,1:T(8,128)(2,1)}), bf16[8192,256]{0,1:T(8,128)(2,1)}) %all-gather.20.cloned.1.call-update) | async-done | bytes 4194320 | tf_op jit(solution)/shard_map/all_gather | solution.py:8
  753.1 4.0 copy.33
  760.9 18.6 %all-gather.6 = bf16[512,256]{1,0:T(8,128)(2,1)S(1)} all-gather(bf16[32,256]{1,0:T(8,128)(2,1)S(1)} %fusion.14), channel_id=8, replica_groups=mesh['leaf'=16,'row'=16] {'leaf'}, dimensions={0}, use_global_device_ids=true | all-gather | bytes 278528 | tf_op jit(solution)/shard_map/all_gather | solution.py:52
  781.8 44.1 %all-gather.22.cloned.1.call-done = bf16[8192,256]{0,1:T(8,128)(2,1)} async-done(((bf16[512,256]{0,1:T(8,128)(2,1)}), bf16[8192,256]{0,1:T(8,128)(2,1)}) %all-gather.22.cloned.1.call-update) | async-done | bytes 4194320 | tf_op jit(solution)/shard_map/all_gather | solution.py:8
  833.7 18.8 %all-gather.8 = bf16[512,256]{1,0:T(8,128)(2,1)S(1)} all-gather(bf16[32,256]{1,0:T(8,128)(2,1)S(1)} %fusion.15), channel_id=10, replica_groups=mesh['leaf'=16,'row'=16] {'leaf'}, dimensions={0}, use_global_device_ids=true | all-gather | bytes 278528 | tf_op jit(solution)/shard_map/all_gather | solution.py:52
  857.5 41.5 %all-gather.24.cloned.1.call-done = bf16[8192,256]{0,1:T(8,128)(2,1)} async-done(((bf16[512,256]{0,1:T(8,128)(2,1)}), bf16[8192,256]{0,1:T(8,128)(2,1)}) %all-gather.24.cloned.1.call-update) | async-done | bytes 4194320 | tf_op jit(solution)/shard_map/all_gather | solution.py:8
  (210 shorter events, 106.4 us)
Async XLA Ops:
  7.2 102.7 %reduce-scatter.16.cloned.1.call-start = ((), (), s32[]{:S(2)}) async-start(), calls=%async_computation.10 | async-start | bytes 278528
  8.1 101.8 %copy-start.30 = (f32[32]{0:T(128)}, f32[32]{0:T(128)S(1)}, u32[]{:S(2)}) copy-start(f32[32]{0:T(128)S(1)} %get-tuple-element.24) | copy-start | bytes 388
  8.1 205.8 %copy-start.32 = (f32[32]{0:T(128)}, f32[32]{0:T(128)S(1)}, u32[]{:S(2)}) copy-start(f32[32]{0:T(128)S(1)} %get-tuple-element.23) | copy-start | bytes 388
  8.1 309.8 %copy-start.34 = (f32[32]{0:T(128)}, f32[32]{0:T(128)S(1)}, u32[]{:S(2)}) copy-start(f32[32]{0:T(128)S(1)} %get-tuple-element.22) | copy-start | bytes 388
  32.5 603.1 %copy-start.39 = (bf16[1,178]{1,0:T(2,128)(2,1)}, bf16[1,178]{1,0:T(2,128)(2,1)S(1)}, u32[]{:S(2)}) copy-start(bf16[1,178]{1,0:T(2,128)(2,1)S(1)} %get-tuple-element.26) | copy-start | bytes 1072
  36.6 73.2 %copy-start.29 = (bf16[6,1,32,256]{3,2,1,0:T(8,128)(2,1)S(1)}, bf16[6,1,32,256]{3,2,1,0:T(8,128)(2,1)}, u32[]{:S(2)}) copy-start(bf16[6,1,32,256]{3,2,1,0:T(8,128)(2,1)} %param.5) | copy-start | bytes 294916
  36.6 177.2 %reduce-scatter.18.cloned.1.call-start = ((), (), s32[]{:S(2)}) async-start(), calls=%async_computation.11 | async-start | bytes 278528
  142.0 175.9 %reduce-scatter.20.cloned.1.call-start = ((), (), s32[]{:S(2)}) async-start(), calls=%async_computation.12 | async-start | bytes 278528
  213.8 23.3 %copy-start.2 = (bf16[1,40,32,512]{3,2,1,0:T(8,128)(2,1)S(1)}, bf16[1,40,32,512]{3,2,1,0:T(8,128)(2,1)}, u32[]{:S(2)}) copy-start(bf16[1,40,32,512]{3,2,1,0:T(8,128)(2,1)} %slice.238) | copy-start | bytes 3932164
  246.0 175.5 %reduce-scatter.22.cloned.1.call-start = ((), (), s32[]{:S(2)}) async-start(), calls=%async_computation.13 | async-start | bytes 278528
  317.8 23.2 %copy-start.7 = (bf16[1,32,32,512]{3,2,1,0:T(8,128)(2,1)S(1)}, bf16[1,32,32,512]{3,2,1,0:T(8,128)(2,1)}, u32[]{:S(2)}) copy-start(bf16[1,32,32,512]{3,2,1,0:T(8,128)(2,1)} %slice.249) | copy-start | bytes 3145732
  349.7 172.7 %reduce-scatter.24.cloned.1.call-start = ((), (), s32[]{:S(2)}) async-start(), calls=%async_computation.14 | async-start | bytes 278528
  350.8 97.1 %copy-start.5 = (bf16[1,16,32,512]{3,2,1,0:T(8,128)(2,1)}, bf16[1,16,32,512]{3,2,1,0:T(8,128)(2,1)S(1)}, u32[]{:S(2)}) copy-start(bf16[1,16,32,512]{3,2,1,0:T(8,128)(2,1)S(1)} %slice.261) | copy-start | bytes 1572868
  450.5 157.3 %all-gather.16.cloned.1.call-start = ((), (), s32[]{:S(2)}) async-start(), calls=%async_computation.5 | async-start | bytes 4456448 | tf_op jit(solution)/shard_map/all_gather | solution.py:8
  522.4 40.8 %copy-start.6 = (bf16[1,16,32,512]{3,2,1,0:T(8,128)(2,1)S(1)}, bf16[1,16,32,512]{3,2,1,0:T(8,128)(2,1)}, u32[]{:S(2)}) copy-start(bf16[1,16,32,512]{3,2,1,0:T(8,128)(2,1)} %copy-done.5) | copy-start | bytes 1572868
  564.2 115.5 %all-gather.18.cloned.1.call-start = ((), (), s32[]{:S(2)}) async-start(), calls=%async_computation.6 | async-start | bytes 4456448 | tf_op jit(solution)/shard_map/all_gather | solution.py:8
  635.5 117.7 %all-gather.20.cloned.1.call-start = ((), (), s32[]{:S(2)}) async-start(), calls=%async_computation.7 | async-start | bytes 4456448 | tf_op jit(solution)/shard_map/all_gather | solution.py:8
  686.3 21.4 %copy-start.3 = (bf16[1,40,32,512]{3,2,1,0:T(8,128)(2,1)S(1)}, bf16[1,40,32,512]{3,2,1,0:T(8,128)(2,1)}, u32[]{:S(2)}) copy-start(bf16[1,40,32,512]{3,2,1,0:T(8,128)(2,1)} %slice.238) | copy-start | bytes 3932164
  708.9 117.0 %all-gather.22.cloned.1.call-start = ((), (), s32[]{:S(2)}) async-start(), calls=%async_computation.8 | async-start | bytes 4456448 | tf_op jit(solution)/shard_map/all_gather | solution.py:8
  757.2 23.0 %copy-start.21 = (bf16[8,32,256]{2,1,0:T(8,128)(2,1)S(1)}, bf16[8,32,256]{2,1,0:T(8,128)(2,1)}, u32[]{:S(2)}) copy-start(bf16[8,32,256]{2,1,0:T(8,128)(2,1)} %copy-done.20) | copy-start | bytes 393220
  757.2 23.0 %copy-start.42 = (bf16[44]{0:T(256)(128)(2,1)S(1)}, bf16[44]{0:T(256)(128)(2,1)}, u32[]{:S(2)}) copy-start(bf16[44]{0:T(256)(128)(2,1)} %slice_bitcast_fusion.1) | copy-start | bytes 268
  781.7 117.4 %all-gather.24.cloned.1.call-start = ((), (), s32[]{:S(2)}) async-start(), calls=%async_computation.9 | async-start | bytes 4456448 | tf_op jit(solution)/shard_map/all_gather | solution.py:8
  830.0 23.4 %copy-start.23 = (bf16[512,256]{1,0:T(8,128)(2,1)S(1)}, bf16[512,256]{1,0:T(8,128)(2,1)}, u32[]{:S(2)}) copy-start(bf16[512,256]{1,0:T(8,128)(2,1)} %copy-done.22) | copy-start | bytes 786436
  857.5 45.6 %copy-start.36 = (bf16[6,32,256]{2,1,0:T(8,128)(2,1)}, bf16[6,32,256]{2,1,0:T(8,128)(2,1)S(1)}, u32[]{:S(2)}) copy-start(bf16[6,32,256]{2,1,0:T(8,128)(2,1)S(1)} %constant_dynamic-update-slice_fusion) | copy-start | bytes 294916
  (29 other events, 74.7 us)
Sparse Core Ops, SparseCore 0:
  36.7 73.0 reduce-scatter.15
  142.1 71.6 reduce-scatter.17
  246.1 71.6 reduce-scatter.19
  349.8 71.6 reduce-scatter.21
  450.6 71.6 reduce-scatter.23
  564.3 43.3 all-gather.15
  635.6 44.0 all-gather.17
  709.1 44.0 all-gather.19
  781.8 44.0 all-gather.21
  855.0 44.0 all-gather.23
